TPU v7x, 32 devices: a whole 2x2x4 slice. The times are simulated.
32 devices in a mesh: dp: 4 (over z), section: 2 (over core), tensor: 4 (over y, x).
Axes of the slice: x: 2, y: 2, z: 4, core: 2. Of those that a mesh axis runs over, the one named last changes fastest.
Arguments:
- tokens: bfloat16 [8, 128, 4096], P('dp', 'tensor'), may hold values from -6 to 6
- segment: int32 [8, 128], P('dp'), may hold values from 0 to 3, never falling along the last dimension, each value on 1 to 64 neighbouring positions
- pack_source: int32 [8], P('dp'), may hold values from 0 to 7, as said below
- norm_gain: float32 [2, 4096], P('section'), may hold values from 0.1 to 1.9
- qkv_weight: bfloat16 [2, 4096, 6144], P('section', None, 'tensor'), may hold values from -3 to 3
- out_weight: bfloat16 [2, 4096, 4096], P('section', 'tensor'), may hold values from -0.1875 to 0.1875
Outputs:
- final_hidden: bfloat16 [8, 128, 4096], P('dp', 'tensor', 'section')
Inputs may be any that keep to these rules, and one draw needn't show every extreme that they name: segment numbers never fall along a pack; each response covers 1 to 64 positions. `pack_source`: each pack number appears once; the 2 slots of one index of dp take packs held by 2 different indices of dp, and the 2 packs held by one index of dp go to slots of 2 different indices of dp.
All inputs are finite; a program needn't handle non-finite values.
Results may differ from a plain program's by a relative error of at most 0.017.
Values may be sent and summed in bfloat16 or wider, within the bound.
A program may use at most 128 MiB of HBM per device.

v0:
```python
import jax
import jax.numpy as jnp
from jax import lax
from jax.sharding import PartitionSpec as P

HD = 128
GROUP = 4


EPSILON = 1e-05
ROPE_BASE = 500000.0


def shifted(value, axis, by):
    size = lax.axis_size(axis)
    pairs = [(i, i + by) for i in range(size) if 0 <= i + by < size]
    return lax.ppermute(value, axis, pairs)


def rotate_pairs(values, cosine, sine_table):
    half_width = values.shape[-1] // 2
    first_half = values[..., :half_width]
    second_half = values[..., half_width:]
    return jnp.concatenate(
        [
            first_half * cosine - second_half * sine_table,
            second_half * cosine + first_half * sine_table,
        ],
        axis=-1,
    )


def rope_tables(segment_ids):
    length = segment_ids.shape[-1]
    earlier = jnp.sum(
        (segment_ids[..., None, :] < segment_ids[..., :, None]).astype(jnp.int32), axis=-1
    )
    position = (jnp.arange(length, dtype=jnp.int32) - earlier).astype(jnp.float32)
    exponent = jnp.arange(0, HD, 2, dtype=jnp.float32) / HD
    frequency = ROPE_BASE ** (-exponent)
    angles = position[..., None] * frequency
    return (jnp.cos(angles), jnp.sin(angles))


def on_device(tokens, segment, pack_source, norm_gain, qkv_weight, out_weight):
    section_count = lax.axis_size("section")
    section_index = lax.axis_index("section")
    micro_count, own_rows, width = tokens.shape
    all_tokens, all_segments = (
        lax.all_gather(tokens, "dp", axis=0, tiled=True),
        lax.all_gather(segment, "dp", axis=0, tiled=True),
    )
    selected = jnp.take(all_tokens, pack_source, axis=0)
    chosen_segments = jnp.take(all_segments, pack_source, axis=0)
    cosine_all, sine_all = rope_tables(chosen_segments)
    pack_length = chosen_segments.shape[1]
    token_order = jnp.arange(pack_length, dtype=jnp.int32)
    gain_row = norm_gain[0]
    weight_in = qkv_weight[0]
    weight_out = out_weight[0]
    local_groups = weight_in.shape[1] // ((GROUP + 2) * HD)
    score_scale = HD ** (-0.5)

    def run_layer(residual, segment_row, cosine_rows, sine_rows):
        mean_square = jnp.mean(residual * residual, axis=-1, keepdims=True)
        normed = (residual * lax.rsqrt(mean_square + EPSILON) * gain_row).astype(jnp.bfloat16)
        piece = lax.all_gather(normed, "tensor", axis=0, tiled=True)
        row_count = piece.shape[0]
        projected = jnp.dot(piece, weight_in, preferred_element_type=jnp.float32).reshape(
            row_count, local_groups, GROUP + 2, HD
        )
        cosine_piece = cosine_rows[:, None, None, :]
        sine_piece = sine_rows[:, None, None, :]
        rotated = rotate_pairs(projected[:, :, : GROUP + 1], cosine_piece, sine_piece)
        joined = jnp.concatenate([rotated, projected[:, :, GROUP + 1 :]], axis=2)
        qkv_rows = (
            joined.astype(jnp.bfloat16)
            .reshape(row_count, local_groups * (GROUP + 2) * HD)
            .reshape(pack_length, local_groups, GROUP + 2, HD)
        )
        queries = qkv_rows[:, :, :GROUP]
        keys_rows = qkv_rows[:, :, GROUP]
        values_rows = qkv_rows[:, :, GROUP + 1]
        allowed = (segment_row[:, None] == segment_row[None, :]) & (
            token_order[None, :] <= token_order[:, None]
        )
        scores = (
            jnp.einsum("qkgd,skd->kgqs", queries, keys_rows, preferred_element_type=jnp.float32)
            * score_scale
        )
        scores = jnp.where(allowed, scores, -1e30)
        largest = jnp.max(scores, axis=-1, keepdims=True)
        exponent_terms = jnp.exp(scores - largest)
        weights = (exponent_terms / jnp.sum(exponent_terms, axis=-1, keepdims=True)).astype(
            jnp.bfloat16
        )
        attended = jnp.einsum(
            "kgqs,skd->qkgd", weights, values_rows, preferred_element_type=jnp.float32
        )
        attended = attended.astype(jnp.bfloat16).reshape(pack_length, local_groups * GROUP * HD)
        return lax.psum_scatter(
            jnp.dot(attended, weight_out, preferred_element_type=jnp.float32).astype(jnp.bfloat16),
            "tensor",
            scatter_dimension=0,
            tiled=True,
        ).astype(jnp.float32)

    def tick(tick_index, loop_state):
        incoming, branches = loop_state
        micro_index = tick_index - section_index
        active = (micro_index >= 0) & (micro_index < micro_count)
        clipped = jnp.clip(micro_index, 0, micro_count - 1)
        fresh_rows = lax.dynamic_index_in_dim(selected, clipped, 0, keepdims=False).astype(
            jnp.float32
        )
        residual = jnp.where(section_index == 0, fresh_rows, incoming)
        segment_row = lax.dynamic_index_in_dim(chosen_segments, clipped, 0, keepdims=False)
        cosine_rows = lax.dynamic_index_in_dim(cosine_all, clipped, 0, keepdims=False)
        sine_rows = lax.dynamic_index_in_dim(sine_all, clipped, 0, keepdims=False)
        branch = run_layer(residual, segment_row, cosine_rows, sine_rows)
        current = lax.dynamic_index_in_dim(branches, clipped, 0, keepdims=False)
        branches = lax.dynamic_update_index_in_dim(
            branches, jnp.where(active, branch, current), clipped, 0
        )
        passed = shifted((residual + branch).astype(jnp.bfloat16), "section", 1).astype(jnp.float32)
        return (passed, branches)

    start_state = (
        jnp.zeros((own_rows, width), jnp.float32),
        jnp.zeros((micro_count, own_rows, width), jnp.float32),
    )
    leftover, branches = lax.fori_loop(0, micro_count + section_count - 1, tick, start_state)
    first_weight = jnp.where(section_index == 0, 1.0, 0.0).astype(jnp.float32)
    contribution = branches + first_weight * selected.astype(jnp.float32)
    summed = lax.psum_scatter(
        contribution.astype(jnp.bfloat16), "section", scatter_dimension=2, tiled=True
    )
    return summed


def solution(mesh):
    placed = (
        P("dp", "tensor", None),
        P("dp", None),
        P("dp"),
        P("section", None),
        P("section", None, "tensor"),
        P("section", "tensor", None),
    )
    return jax.shard_map(
        on_device,
        mesh=mesh,
        in_specs=placed,
        out_specs=P("dp", "tensor", "section"),
        check_vma=False,
    )
```

profile of v0, /device:TPU:1, one launch (start us, length us, event | category | flops | bytes accessed | tf_op | source)
XLA Modules:
  0.0 323.9 jit_solution(17589053785045567385)
XLA Ops:
  7.3 10.2 %all-gather = s32[4,2,128]{2,1,0:T(2,128)S(1)} all-gather(s32[1,2,128]{2,1,0:T(2,128)} %bitcast.115), channel_id=1, replica_groups=mesh['dp'=4,'section'=2,'tensor'=4] {'dp'}, dimensions={0}, use_global_device_ids=true | all-gather | bytes 5120 | tf_op jit(solution)/shard_map/all_gather | solution.py:51
  22.1 34.9 %all-gather.4.cloned.1.call-done = bf16[8,32,4096]{2,1,0:T(8,128)(2,1)} async-done(((bf16[2,32,4096]{2,1,0:T(8,128)(2,1)}), bf16[8,32,4096]{2,1,0:T(8,128)(2,1)}) %all-gather.4.cloned.1.call-update) | async-done | bytes 2097168 | tf_op jit(solution)/shard_map/all_gather | solution.py:50
  57.0 2.2 gather_fusion
  60.4 245.0 %while.17 = (s32[]{:T(128)}, f32[32,4096]{1,0:T(8,128)S(1)}, f32[2,32,4096]{2,1,0:T(8,128)}, pred[]{:T(512)}, s32[]{:T(128)}, /*index=5*/bf16[2,32,4096]{2,1,0:T...) while((s32[]{:T(128)}, f32[32,4096]{1,0:T(8,128)S(1)}, ...), condition=%wide.region_6.7_spmd.clone, body=%wide.region_1.6_spmd.clone.sunk | while | flops 2791490816 | bytes 54208956 | solution.py:132
  64.5 24.1 %all-gather.6.cloned.1.call-done = bf16[128,4096]{1,0:T(8,128)(2,1)} async-done(((bf16[32,4096]{1,0:T(8,128)(2,1)}), bf16[128,4096]{1,0:T(8,128)(2,1)}) %all-gather.6.cloned.1.call-update) | async-done | bytes 1048592 | tf_op jit(solution)/shard_map/while/body/eval_jaxpr/all_gather | solution.py:67
  88.6 8.3 %fusion.58 = f32[128,1536]{0,1:T(8,128)S(1)} fusion(bf16[128,4096]{1,0:T(8,128)(2,1)} %all-gather.6.cloned.1.call-done, bf16[4096,1536]{1,0:T(8,128)(2,1)} %get-tuple-element.453), kind=kOutput, calls=%fused_computation.59.clone.1 | convolution fusion | flops 1610612736 | bytes 14417920 | tf_op jit(solution)/shard_map/while/body/eval_jaxpr/dot_general | solution.py:69
  97.4 1.8 subtract_convert_fusion.3
  101.3 1.8 convolution_convert_fusion.4
  103.1 5.6 %convolution_convert_fusion.5 = bf16[128,4096]{1,0:T(8,128)(2,1)} fusion(bf16[128,1024]{0,1:T(8,128)(2,1)S(1)} %bitcast.112, bf16[1024,4096]{1,0:T(8,128)(2,1)} %get-tuple-element.457), kind=kOutput, calls=%fused_computation.4.clone.1 | convolution fusion | flops 1074266112 | bytes 9699328 | tf_op jit(solution)/shard_map/while/body/eval_jaxpr/dot_general | solution.py:102
  108.9 27.8 %reduce-scatter.5.cloned.1.call-done = bf16[32,4096]{1,0:T(8,128)(2,1)} async-done(((bf16[128,4096]{1,0:T(8,128)(2,1)}), bf16[32,4096]{1,0:T(8,128)(2,1)}) %reduce-scatter.5.cloned.1.call-update) | async-done | bytes 262160 | tf_op jit(solution)/shard_map/while/body/eval_jaxpr/reduce_scatter | solution.py:101
  145.3 25.3 %all-gather.6.cloned.1.call-done = bf16[128,4096]{1,0:T(8,128)(2,1)} async-done(((bf16[32,4096]{1,0:T(8,128)(2,1)}), bf16[128,4096]{1,0:T(8,128)(2,1)}) %all-gather.6.cloned.1.call-update) | async-done | bytes 1048592 | tf_op jit(solution)/shard_map/while/body/eval_jaxpr/all_gather | solution.py:67
  170.7 8.3 %fusion.58 = f32[128,1536]{0,1:T(8,128)S(1)} fusion(bf16[128,4096]{1,0:T(8,128)(2,1)} %all-gather.6.cloned.1.call-done, bf16[4096,1536]{1,0:T(8,128)(2,1)} %get-tuple-element.453), kind=kOutput, calls=%fused_computation.59.clone.1 | convolution fusion | flops 1610612736 | bytes 14417920 | tf_op jit(solution)/shard_map/while/body/eval_jaxpr/dot_general | solution.py:69
  179.5 1.8 subtract_convert_fusion.3
  183.4 1.8 convolution_convert_fusion.4
  185.2 5.6 %convolution_convert_fusion.5 = bf16[128,4096]{1,0:T(8,128)(2,1)} fusion(bf16[128,1024]{0,1:T(8,128)(2,1)S(1)} %bitcast.112, bf16[1024,4096]{1,0:T(8,128)(2,1)} %get-tuple-element.457), kind=kOutput, calls=%fused_computation.4.clone.1 | convolution fusion | flops 1074266112 | bytes 9699328 | tf_op jit(solution)/shard_map/while/body/eval_jaxpr/dot_general | solution.py:102
  190.9 27.8 %reduce-scatter.5.cloned.1.call-done = bf16[32,4096]{1,0:T(8,128)(2,1)} async-done(((bf16[128,4096]{1,0:T(8,128)(2,1)}), bf16[32,4096]{1,0:T(8,128)(2,1)}) %reduce-scatter.5.cloned.1.call-update) | async-done | bytes 262160 | tf_op jit(solution)/shard_map/while/body/eval_jaxpr/reduce_scatter | solution.py:101
  227.4 25.3 %all-gather.6.cloned.1.call-done = bf16[128,4096]{1,0:T(8,128)(2,1)} async-done(((bf16[32,4096]{1,0:T(8,128)(2,1)}), bf16[128,4096]{1,0:T(8,128)(2,1)}) %all-gather.6.cloned.1.call-update) | async-done | bytes 1048592 | tf_op jit(solution)/shard_map/while/body/eval_jaxpr/all_gather | solution.py:67
  252.7 8.3 %fusion.58 = f32[128,1536]{0,1:T(8,128)S(1)} fusion(bf16[128,4096]{1,0:T(8,128)(2,1)} %all-gather.6.cloned.1.call-done, bf16[4096,1536]{1,0:T(8,128)(2,1)} %get-tuple-element.453), kind=kOutput, calls=%fused_computation.59.clone.1 | convolution fusion | flops 1610612736 | bytes 14417920 | tf_op jit(solution)/shard_map/while/body/eval_jaxpr/dot_general | solution.py:69
  261.6 1.8 subtract_convert_fusion.3
  265.5 1.8 convolution_convert_fusion.4
  267.3 5.6 %convolution_convert_fusion.5 = bf16[128,4096]{1,0:T(8,128)(2,1)} fusion(bf16[128,1024]{0,1:T(8,128)(2,1)S(1)} %bitcast.112, bf16[1024,4096]{1,0:T(8,128)(2,1)} %get-tuple-element.457), kind=kOutput, calls=%fused_computation.4.clone.1 | convolution fusion | flops 1074266112 | bytes 9699328 | tf_op jit(solution)/shard_map/while/body/eval_jaxpr/dot_general | solution.py:102
  273.0 27.8 %reduce-scatter.5.cloned.1.call-done = bf16[32,4096]{1,0:T(8,128)(2,1)} async-done(((bf16[128,4096]{1,0:T(8,128)(2,1)}), bf16[32,4096]{1,0:T(8,128)(2,1)}) %reduce-scatter.5.cloned.1.call-update) | async-done | bytes 262160 | tf_op jit(solution)/shard_map/while/body/eval_jaxpr/reduce_scatter | solution.py:101
  305.4 2.4 add_convert_fusion.1
  307.9 9.2 %reduce-scatter.3.cloned.1.call-done = bf16[2,32,2048]{2,1,0:T(8,128)(2,1)} async-done(((bf16[2,32,4096]{2,1,0:T(8,128)(2,1)}), bf16[2,32,2048]{2,1,0:T(8,128)(2,1)}) %reduce-scatter.3.cloned.1.call-update) | async-done | bytes 262160 | tf_op jit(solution)/shard_map/reduce_scatter | solution.py:135
  (98 shorter events, 40.5 us)
Async XLA Ops:
  6.5 50.4 %all-gather.4.cloned.1.call-start = ((), (), s32[]{:S(2)}) async-start(), calls=%async_computation.2 | async-start | bytes 2621440 | tf_op jit(solution)/shard_map/all_gather | solution.py:50
  19.4 41.0 %copy-start.4 = (pred[2]{0:T(512)(128)(4,1)}, pred[2]{0:T(512)(128)(4,1)S(1)}, u32[]{:S(2)}) copy-start(pred[2]{0:T(512)(128)(4,1)S(1)} %compare_and_fusion) | copy-start | bytes 10
  59.2 1.2 copy-start.3
  60.4 28.2 %all-gather.6.cloned.1.call-start = ((), (), s32[]{:S(2)}) async-start(), calls=%async_computation.4 | async-start | bytes 1310720 | tf_op jit(solution)/shard_map/while/body/eval_jaxpr/all_gather | solution.py:67
  62.2 74.5 %reduce-scatter.5.cloned.1.call-start = ((), (), s32[]{:S(2)}) async-start(), calls=%async_computation.5 | async-start | bytes 1310720 | tf_op jit(solution)/shard_map/while/body/eval_jaxpr/reduce_scatter | solution.py:101
  99.2 0.7 copy-start.2
  101.3 7.5 %copy-start = (f32[2,32,4096]{2,1,0:T(8,128)S(1)}, f32[2,32,4096]{2,1,0:T(8,128)}, u32[]{:S(2)}) copy-start(f32[2,32,4096]{2,1,0:T(8,128)} %get-tuple-element.433) | copy-start | bytes 3145732 | tf_op jit(solution)/shard_map/while
  137.7 3.4 %collective-permute-start = (bf16[32,4096]{1,0:T(8,128)(2,1)S(1)}, bf16[32,4096]{1,0:T(8,128)(2,1)S(1)}, u32[]{:S(2)}, u32[]{:S(2)}) collective-permute-start(bf16[32,4096]{1,0:T(8,128)(2,1)S(1)} %fusion.63), channel_id=1, source_target_pairs={{0,4},{1,5},{2,6},{3,7},{8,12},{9,13},{10,14},{11,15},{16,20},{17,... | collective-permute-start | bytes 786440 | tf_op jit(solution)/shard_map/while/body/eval_jaxpr/ppermute | solution.py:17
  140.0 1.2 copy-start.1
  141.2 29.5 %all-gather.6.cloned.1.call-start = ((), (), s32[]{:S(2)}) async-start(), calls=%async_computation.4 | async-start | bytes 1310720 | tf_op jit(solution)/shard_map/while/body/eval_jaxpr/all_gather | solution.py:67
  143.1 75.7 %reduce-scatter.5.cloned.1.call-start = ((), (), s32[]{:S(2)}) async-start(), calls=%async_computation.5 | async-start | bytes 1310720 | tf_op jit(solution)/shard_map/while/body/eval_jaxpr/reduce_scatter | solution.py:101
  181.3 0.7 copy-start.2
  183.4 7.5 %copy-start = (f32[2,32,4096]{2,1,0:T(8,128)S(1)}, f32[2,32,4096]{2,1,0:T(8,128)}, u32[]{:S(2)}) copy-start(f32[2,32,4096]{2,1,0:T(8,128)} %get-tuple-element.433) | copy-start | bytes 3145732 | tf_op jit(solution)/shard_map/while
  219.8 3.4 %collective-permute-start = (bf16[32,4096]{1,0:T(8,128)(2,1)S(1)}, bf16[32,4096]{1,0:T(8,128)(2,1)S(1)}, u32[]{:S(2)}, u32[]{:S(2)}) collective-permute-start(bf16[32,4096]{1,0:T(8,128)(2,1)S(1)} %fusion.63), channel_id=1, source_target_pairs={{0,4},{1,5},{2,6},{3,7},{8,12},{9,13},{10,14},{11,15},{16,20},{17,... | collective-permute-start | bytes 786440 | tf_op jit(solution)/shard_map/while/body/eval_jaxpr/ppermute | solution.py:17
  222.1 1.2 copy-start.1
  223.3 29.4 %all-gather.6.cloned.1.call-start = ((), (), s32[]{:S(2)}) async-start(), calls=%async_computation.4 | async-start | bytes 1310720 | tf_op jit(solution)/shard_map/while/body/eval_jaxpr/all_gather | solution.py:67
  225.1 75.7 %reduce-scatter.5.cloned.1.call-start = ((), (), s32[]{:S(2)}) async-start(), calls=%async_computation.5 | async-start | bytes 1310720 | tf_op jit(solution)/shard_map/while/body/eval_jaxpr/reduce_scatter | solution.py:101
  263.3 0.7 copy-start.2
  265.5 7.5 %copy-start = (f32[2,32,4096]{2,1,0:T(8,128)S(1)}, f32[2,32,4096]{2,1,0:T(8,128)}, u32[]{:S(2)}) copy-start(f32[2,32,4096]{2,1,0:T(8,128)} %get-tuple-element.433) | copy-start | bytes 3145732 | tf_op jit(solution)/shard_map/while
  301.9 3.4 %collective-permute-start = (bf16[32,4096]{1,0:T(8,128)(2,1)S(1)}, bf16[32,4096]{1,0:T(8,128)(2,1)S(1)}, u32[]{:S(2)}, u32[]{:S(2)}) collective-permute-start(bf16[32,4096]{1,0:T(8,128)(2,1)S(1)} %fusion.63), channel_id=1, source_target_pairs={{0,4},{1,5},{2,6},{3,7},{8,12},{9,13},{10,14},{11,15},{16,20},{17,... | collective-permute-start | bytes 786440 | tf_op jit(solution)/shard_map/while/body/eval_jaxpr/ppermute | solution.py:17
  304.2 1.2 copy-start.1
  305.4 11.7 %reduce-scatter.3.cloned.1.call-start = ((), (), s32[]{:S(2)}) async-start(), calls=%async_computation.3 | async-start | bytes 786432 | tf_op jit(solution)/shard_map/reduce_scatter | solution.py:135
Sparse Core Ops, SparseCore 0:
  8.9 48.0 all-gather.3
  63.2 25.3 all-gather.5
  108.9 27.7 reduce-scatter.4
  143.7 26.8 all-gather.5
  191.0 27.7 reduce-scatter.4
  225.8 26.8 all-gather.5
  273.1 27.7 reduce-scatter.4
  308.4 8.5 reduce-scatter.2
where the time goes:
time: 325 us; the launch traced here: 324 us
  waiting for transfers between devices  206 us (63%)
  matrix products  51.4 us (16%)
  other arithmetic  23.6 us (7%)
  local copies, waits for them, and re-layouts  14.1 us (4%)
  between operations  13.5 us (4%)
  blocking collectives  10.2 us (3%)
  starting transfers between devices  4.14 us (1%)
    reduce_scatter x3, waiting for transfers between devices, run_layer(): lax.psum_scatter(jnp.dot(attended, weight_out, preferred_element_type=jnp...  83.4 us
    all_gather x3, waiting for transfers between devices, run_layer(): piece = lax.all_gather(normed, 'tensor', axis=0, tiled=True)  74.8 us
    all_gather x1, waiting for transfers between devices, on_device(): lax.all_gather(tokens, 'dp', axis=0, tiled=True)  34.9 us
    dot_general x3, matrix products, run_layer(): jnp.dot(piece, weight_in, preferred_element_type=jnp.float32)  24.9 us
    dot_general x3, matrix products, run_layer(): jnp.dot(attended, weight_out, preferred_element_type=jnp.float32)  16.9 us
    all_gather x1, blocking collectives, on_device(): lax.all_gather(segment, 'dp', axis=0, tiled=True)  10.2 us
    reduce_scatter x1, waiting for transfers between devices, on_device(): lax.psum_scatter(contribution.astype(jnp.bfloat16), 'section', scatter_di...  9.2 us
  transfers between devices with their start and end apart: 11, of which 11 were waited for; matrix products, arithmetic and copies ran while one was open for 4% of the time, Pallas kernels for 0%

commit v1 on v0

v1 whole, which is shorter than its diff:
```python
import functools

import jax
import jax.numpy as jnp
from jax import lax
from jax.experimental import pallas as pl
from jax.experimental.pallas import tpu as pltpu
from jax.sharding import PartitionSpec as P

HD = 128
GROUP = 4
EPSILON = 1e-05
ROPE_BASE = 500000.0
CHUNKS = 4
MESH = pl.DeviceIdType.MESH


def kernel(
    dp_count,
    tensor_count,
    frequency_ref,
    source_ref,
    segment_ref,
    tokens_ref,
    gain_ref,
    qkv_hbm,
    out_hbm,
    result_ref,
    weight_in,
    weight_out,
    meta,
    sent_packs,
    held_packs,
    gathered,
    hidden,
    hidden_low,
    normed,
    projected,
    square_sum,
    attended,
    partial,
    arrived,
    cosine,
    sine,
    bias,
    weight_sem,
    meta_send,
    meta_recv,
    pack_send,
    pack_recv,
    gather_send,
    gather_recv,
    next_send,
    sum_send,
    sum_recv,
):
    micro, rows, width = tokens_ref.shape
    length = segment_ref.shape[1]
    part = width // CHUNKS
    half = CHUNKS // 2
    z = lax.axis_index("dp")
    section = lax.axis_index("section")
    me = lax.axis_index("tensor")
    groups = weight_in.shape[2] // ((GROUP + 2) * HD)

    weight_copies = [
        pltpu.make_async_copy(
            qkv_hbm.at[0, pl.ds(c * part, part), :], weight_in.at[c], weight_sem.at[c]
        )
        for c in range(CHUNKS)
    ] + [
        pltpu.make_async_copy(
            out_hbm.at[0, :, pl.ds(c * part, part)], weight_out.at[c], weight_sem.at[CHUNKS + c]
        )
        for c in range(CHUNKS)
    ]
    for copy in weight_copies:
        copy.start()

    for i in range(micro):
        meta[z, i : i + 1, :] = segment_ref[i : i + 1, :]
        meta[z, micro + i : micro + i + 1, :] = jnp.full((1, length), source_ref[i], jnp.int32)

    barrier = pltpu.get_barrier_semaphore()

    @pl.loop(1, dp_count)
    def _(off):
        pl.semaphore_signal(
            barrier, inc=1, device_id={"dp": lax.rem(z + off, dp_count)}, device_id_type=MESH
        )

    for off in range(tensor_count):
        for other in range(2):
            if off == 0 and other == 0:
                continue
            pl.semaphore_signal(
                barrier,
                inc=1,
                device_id={
                    "tensor": lax.rem(me + off, tensor_count),
                    "section": lax.rem(section + other, 2),
                },
                device_id_type=MESH,
            )
    pl.semaphore_wait(barrier, dp_count - 1 + 2 * tensor_count - 1)

    def meta_copy(off):
        return pltpu.make_async_remote_copy(
            src_ref=meta.at[z],
            dst_ref=meta.at[z],
            send_sem=meta_send.at[off],
            recv_sem=meta_recv.at[off],
            device_id={"dp": lax.rem(z + off, dp_count)},
            device_id_type=MESH,
        )

    @pl.loop(1, dp_count)
    def _(off):
        meta_copy(off).start()

    @pl.loop(1, dp_count)
    def _(off):
        copy = meta_copy(off)
        copy.wait_send()
        copy.wait_recv()

    def pack_copy(c, off):
        target = lax.rem(z + off, dp_count)
        return pltpu.make_async_remote_copy(
            src_ref=sent_packs.at[c, target],
            dst_ref=held_packs.at[c, z],
            send_sem=pack_send.at[c, off],
            recv_sem=pack_recv.at[c, off],
            device_id={"dp": target},
            device_id_type=MESH,
        )

    def gather_copy(p, c, off):
        return pltpu.make_async_remote_copy(
            src_ref=gathered.at[p, c, pl.ds(pl.multiple_of(me * rows, rows), rows), :],
            dst_ref=gathered.at[p, c, pl.ds(pl.multiple_of(me * rows, rows), rows), :],
            send_sem=gather_send.at[p, c, off],
            recv_sem=gather_recv.at[p, c, off],
            device_id={"tensor": lax.rem(me + off, tensor_count)},
            device_id_type=MESH,
        )

    def next_copy(p, c, off):
        return pltpu.make_async_remote_copy(
            src_ref=hidden_low.at[p, c],
            dst_ref=gathered.at[p, c, pl.ds(pl.multiple_of(me * rows, rows), rows), :],
            send_sem=next_send.at[p, c, off],
            recv_sem=gather_recv.at[p, c, off],
            device_id={"tensor": lax.rem(me + off, tensor_count), "section": 1},
            device_id_type=MESH,
        )

    def wide(row):
        return jnp.concatenate([row] * (part // length), axis=1) if part > length else row[:, :part]

    @pl.when(section == 0)
    def _():
        @pl.loop(0, CHUNKS)
        def _(c):
            columns = pl.ds(pl.multiple_of(c * part, part), part)

            def choose(target):
                total = jnp.zeros((rows, part), jnp.float32)
                for k in range(micro):
                    wanted = jnp.zeros((1, length), jnp.float32)
                    for i in range(micro):
                        row = meta[target, micro + i : micro + i + 1, :]
                        wanted = wanted + jnp.where(row == z * micro + k, 1.0, 0.0)
                    total = total + tokens_ref[k, :, columns].astype(jnp.float32) * wide(wanted)
                return total.astype(jnp.bfloat16)

            held_packs[c, z] = choose(z)

            @pl.loop(1, dp_count)
            def _(off):
                target = lax.rem(z + off, dp_count)
                sent_packs[c, target] = choose(target)
                pack_copy(c, off).start()

    freq = frequency_ref[0:1, :]
    row_id = lax.broadcasted_iota(jnp.int32, (length, length), 0)
    column_id = lax.broadcasted_iota(jnp.int32, (length, length), 1)
    lane = lax.broadcasted_iota(jnp.int32, (length, HD), 1)
    for p in range(micro):
        own = meta[z, micro + p : micro + p + 1, :]

        def add_segment(holder, total, own=own):
            for k in range(micro):
                row = meta[holder, k : k + 1, :]
                total = total + jnp.where(own == holder * micro + k, row, 0)
            return total

        chosen = lax.fori_loop(0, dp_count, add_segment, jnp.zeros((1, length), jnp.int32))
        across = jnp.broadcast_to(chosen.astype(jnp.float32), (length, length))
        down = across.T
        earlier = jnp.sum(jnp.where(across < down, 1.0, 0.0), axis=1, keepdims=True)
        order = lax.broadcasted_iota(jnp.int32, (length, 1), 0).astype(jnp.float32)
        angle = (order - earlier) * freq
        cosine[p] = jnp.cos(angle)
        sine[p] = jnp.where(lane < HD // 2, -1.0, 1.0) * jnp.sin(angle)
        bias[p] = jnp.where((across == down) & (column_id <= row_id), 0.0, -1e30)

    @pl.when(section == 0)
    def _():
        @pl.loop(0, CHUNKS)
        def _(c):
            @pl.loop(1, dp_count)
            def _(off):
                pack_copy(c, off).wait_recv()

            for p in range(micro):
                own = meta[z, micro + p : micro + p + 1, :]

                def add_pack(holder, total, own=own):
                    hit = jnp.where((own >= holder * micro) & (own < (holder + 1) * micro), 1.0, 0.0)
                    return total + held_packs[c, holder].astype(jnp.float32) * wide(hit)

                picked = lax.fori_loop(
                    0, dp_count, add_pack, jnp.zeros((rows, part), jnp.float32)
                )
                hidden[p, c] = picked
                gathered[p, c, pl.ds(pl.multiple_of(me * rows, rows), rows), :] = picked.astype(
                    jnp.bfloat16
                )
                for off in range(1, tensor_count):
                    gather_copy(p, c, off).start()

    for copy in weight_copies:
        copy.wait()

    def sum_copy(p, c, off):
        target = lax.rem(me + off, tensor_count)
        place = c + section * (CHUNKS + c % half - c)
        return dict(
            src_ref=partial.at[p, c, pl.ds(pl.multiple_of(target * rows, rows), rows), :],
            dst_ref=arrived.at[p, place, me],
            to=(target, section * (c // half)),
            send_sem=sum_send.at[p, c, off],
            recv_sem=sum_recv.at[p, place, off],
        )

    def sum_remote(p, c, off):
        d = sum_copy(p, c, off)
        return pltpu.make_async_remote_copy(
            src_ref=d["src_ref"],
            dst_ref=d["dst_ref"],
            send_sem=d["send_sem"],
            recv_sem=d["recv_sem"],
            device_id={"tensor": d["to"][0], "section": d["to"][1]},
            device_id_type=MESH,
        )

    def rotate(x, p):
        return x * cosine[p] + pltpu.roll(x, HD // 2, 1) * sine[p]

    @pl.loop(0, micro)
    def _(p):
        @pl.loop(0, CHUNKS)
        def _(c):
            @pl.when(section == 1)
            def _():
                next_copy(p, c, 0).wait_recv()

            for off in range(1, tensor_count):
                gather_copy(p, c, off).wait_recv()
            block = gathered[p, c].astype(jnp.float32)
            squares = jnp.sum(block * block, axis=1, keepdims=True)
            normed[...] = (
                block * gain_ref[0:1, pl.ds(pl.multiple_of(c * part, part), part)]
            ).astype(jnp.bfloat16)
            total_columns = weight_in.shape[2]
            tile = 256

            @pl.when(c == 0)
            def _():
                square_sum[...] = jnp.broadcast_to(squares, square_sum.shape)
                for n in range(0, total_columns, tile):
                    projected[:, n : n + tile] = jnp.dot(
                        normed[...],
                        weight_in[c, :, n : n + tile],
                        preferred_element_type=jnp.float32,
                    )

            @pl.when(c > 0)
            def _():
                square_sum[...] += jnp.broadcast_to(squares, square_sum.shape)
                for n in range(0, total_columns, tile):
                    projected[:, n : n + tile] += jnp.dot(
                        normed[...],
                        weight_in[c, :, n : n + tile],
                        preferred_element_type=jnp.float32,
                    )

        scale = lax.rsqrt(square_sum[...] * (1.0 / width) + EPSILON)
        for g in range(groups):
            base = g * (GROUP + 2) * HD
            at = base + GROUP * HD
            key = rotate(projected[:, at : at + HD] * scale, p).astype(jnp.bfloat16)
            at = at + HD
            value = (projected[:, at : at + HD] * scale).astype(jnp.bfloat16)
            for h in range(GROUP):
                at = base + h * HD
                query = rotate(projected[:, at : at + HD] * scale, p).astype(jnp.bfloat16)
                scores = lax.dot_general(
                    query, key, (((1,), (1,)), ((), ())), preferred_element_type=jnp.float32
                )
                scores = jnp.where(bias[p] < 0.0, -1e30, scores * HD ** (-0.5))
                terms = jnp.exp(scores - jnp.max(scores, axis=1, keepdims=True))
                weights = (terms / jnp.sum(terms, axis=1, keepdims=True)).astype(jnp.bfloat16)
                at = (g * GROUP + h) * HD
                attended[:, at : at + HD] = jnp.dot(
                    weights, value, preferred_element_type=jnp.float32
                ).astype(jnp.bfloat16)

        @pl.loop(0, CHUNKS)
        def _(c):
            tile = min(256, part)
            for n in range(0, part, tile):
                partial[p, c, :, n : n + tile] = jnp.dot(
                    attended[...],
                    weight_out[c, :, n : n + tile],
                    preferred_element_type=jnp.float32,
                ).astype(jnp.bfloat16)
            for off in range(1, tensor_count):
                sum_remote(p, c, off).start()

            @pl.when(section * (c // half) == section)
            def _():
                d = sum_copy(p, c, 0)
                pltpu.make_async_copy(d["src_ref"], d["dst_ref"], d["recv_sem"]).start()

            @pl.when(section * (c // half) != section)
            def _():
                sum_remote(p, c, 0).start()

    def wait_sums(p, place):
        for off in range(tensor_count):
            pltpu.make_async_copy(
                arrived.at[p, place, lax.rem(me + tensor_count - off, tensor_count)],
                arrived.at[p, place, lax.rem(me + tensor_count - off, tensor_count)],
                sum_recv.at[p, place, off],
            ).wait()

    def add_up(p, place):
        total = arrived[p, place, 0].astype(jnp.float32)
        for t in range(1, tensor_count):
            total = total + arrived[p, place, t].astype(jnp.float32)
        return total

    @pl.when(section == 0)
    def _():
        @pl.loop(0, micro)
        def _(p):
            @pl.loop(0, CHUNKS)
            def _(c):
                wait_sums(p, c)
                after = hidden[p, c] + add_up(p, c)
                hidden[p, c] = after
                hidden_low[p, c] = after.astype(jnp.bfloat16)
                for off in range(tensor_count):
                    next_copy(p, c, off).start()

    @pl.when(section == 1)
    def _():
        for p in range(micro):
            for j in range(half):
                hidden[p, j] = gathered[
                    p, half + j, pl.ds(pl.multiple_of(me * rows, rows), rows), :
                ].astype(jnp.float32)

    @pl.loop(0, micro)
    def _(p):
        for j in range(half):
            wait_sums(p, CHUNKS + j)
            result_ref[p, :, j * part : (j + 1) * part] = (
                hidden[p, j] + add_up(p, CHUNKS + j)
            ).astype(jnp.bfloat16)

    @pl.loop(0, micro)
    def _(p):
        @pl.loop(0, CHUNKS)
        def _(c):
            for off in range(1, tensor_count):
                sum_remote(p, c, off).wait_send()

            @pl.when(section * (c // half) != section)
            def _():
                sum_remote(p, c, 0).wait_send()

            @pl.when(section == 0)
            def _():
                for off in range(1, tensor_count):
                    gather_copy(p, c, off).wait_send()
                for off in range(tensor_count):
                    next_copy(p, c, off).wait_send()

    @pl.when(section == 0)
    def _():
        @pl.loop(0, CHUNKS)
        def _(c):
            @pl.loop(1, dp_count)
            def _(off):
                pack_copy(c, off).wait_send()


def on_device(tokens, segment, pack_source, norm_gain, qkv_weight, out_weight):
    dp_count = lax.axis_size("dp")
    tensor_count = lax.axis_size("tensor")
    micro, rows, width = tokens.shape
    length = segment.shape[1]
    part = width // CHUNKS
    columns = qkv_weight.shape[2]
    depth = out_weight.shape[1]
    places = CHUNKS + CHUNKS // 2
    exponent = jnp.arange(0, HD, 2, dtype=jnp.float32) / HD
    frequency = ROPE_BASE ** (-exponent)
    frequency = jnp.concatenate([frequency, frequency])[None, :]
    vmem = pl.BlockSpec(memory_space=pltpu.VMEM)
    anywhere = pl.BlockSpec(memory_space=pl.ANY)
    dma = pltpu.SemaphoreType.DMA
    bf16, f32 = jnp.bfloat16, jnp.float32
    return pl.pallas_call(
        functools.partial(kernel, dp_count, tensor_count),
        out_shape=jax.ShapeDtypeStruct((micro, rows, width // 2), bf16),
        in_specs=[
            vmem,
            pl.BlockSpec(memory_space=pltpu.SMEM),
            vmem,
            vmem,
            vmem,
            anywhere,
            anywhere,
        ],
        out_specs=vmem,
        scratch_shapes=[
            pltpu.VMEM((CHUNKS, part, columns), bf16),
            pltpu.VMEM((CHUNKS, depth, part), bf16),
            pltpu.VMEM((dp_count, 8, length), jnp.int32),
            pltpu.VMEM((CHUNKS, dp_count, rows, part), bf16),
            pltpu.VMEM((CHUNKS, dp_count, rows, part), bf16),
            pltpu.VMEM((micro, CHUNKS, length, part), bf16),
            pltpu.VMEM((micro, CHUNKS, rows, part), f32),
            pltpu.VMEM((micro, CHUNKS, rows, part), bf16),
            pltpu.VMEM((length, part), bf16),
            pltpu.VMEM((length, columns), f32),
            pltpu.VMEM((length, HD), f32),
            pltpu.VMEM((length, depth), bf16),
            pltpu.VMEM((micro, CHUNKS, length, part), bf16),
            pltpu.VMEM((micro, places, tensor_count, rows, part), bf16),
            pltpu.VMEM((micro, length, HD), f32),
            pltpu.VMEM((micro, length, HD), f32),
            pltpu.VMEM((micro, length, length), f32),
            dma((2 * CHUNKS,)),
            dma((dp_count,)),
            dma((dp_count,)),
            dma((CHUNKS, dp_count)),
            dma((CHUNKS, dp_count)),
            dma((micro, CHUNKS, tensor_count)),
            dma((micro, CHUNKS, tensor_count)),
            dma((micro, CHUNKS, tensor_count)),
            dma((micro, CHUNKS, tensor_count)),
            dma((micro, places, tensor_count)),
        ],
        compiler_params=pltpu.CompilerParams(
            collective_id=0, has_side_effects=True, vmem_limit_bytes=58 * 1024 * 1024
        ),
    )(frequency, pack_source, segment, tokens, norm_gain, qkv_weight, out_weight)


def solution(mesh):
    placed = (
        P("dp", "tensor", None),
        P("dp", None),
        P("dp"),
        P("section", None),
        P("section", None, "tensor"),
        P("section", "tensor", None),
    )
    return jax.shard_map(
        on_device,
        mesh=mesh,
        in_specs=placed,
        out_specs=P("dp", "tensor", "section"),
        check_vma=False,
    )
```

time: 325 us -> 80 us (0.25)
  waiting for transfers between devices: 206 us -> 0 us
  Pallas kernels: 0 us -> 77.6 us
  matrix products: 51.4 us -> 0 us
  other arithmetic: 23.6 us -> 0.6 us
  between operations: 13.5 us -> 0.01 us
  local copies, waits for them, and re-layouts: 14.1 us -> 1.67 us
  blocking collectives: 10.2 us -> 0 us
  starting transfers between devices: 4.14 us -> 0 us
    all_gather x4 -> x0, waiting for transfers between devices: 110 us -> none  [the longest x3 74.8 us: run_layer(): piece = lax.all_gather(normed, 'tensor', axis=0, tiled=True)]
    reduce_scatter x4 -> x0, waiting for transfers between devices: 92.6 us -> none  [the longest x3 83.4 us: run_layer(): lax.psum_scatter(jnp.dot(attended, weight_out, preferred_element_type=jnp...]
    pallas_call x0 -> x1, Pallas kernels: none -> 77.6 us  [on_device(): pl.pallas_call(functools.partial(kernel, dp_count, tensor_count), out_sha...]
    dot_general x9 -> x0, matrix products: 47.1 us -> none  [the longest x3 24.9 us: run_layer(): jnp.dot(piece, weight_in, preferred_element_type=jnp.float32)]
    convert_element_type x11 -> x0, other arithmetic: 10.3 us -> none  [the longest x3 4.63 us: run_layer(): (residual * lax.rsqrt(mean_square + EPSILON) * gain_row).astype(jnp.bfloa...]
    all_gather x1 -> x0, blocking collectives: 10.2 us -> none  [on_device(): lax.all_gather(segment, 'dp', axis=0, tiled=True)]
    another operation x3 -> x0, other arithmetic: 5.25 us -> none
    mul x3 -> x0, local copies, waits for them, and re-layouts: 4.52 us -> none  [rotate_pairs(): second_half * sine_table]
  transfers between devices with their start and end apart: 11 -> 0, of which waited for: 11 -> 0; matrix products, arithmetic and copies ran while one was open for 4% -> 0% of each run, Pallas kernels for 0% -> 0%
where the time goes in v1:
time: 80 us; the launch traced here: 79.9 us
  Pallas kernels  77.6 us (97%)
  local copies, waits for them, and re-layouts  1.67 us (2%)
    pallas_call x1, Pallas kernels, on_device(): pl.pallas_call(functools.partial(kernel, dp_count, tensor_count), out_sha...  77.6 us
    unnamed x1, local copies, waits for them, and re-layouts  1.67 us

profile of v1, /device:TPU:1, one launch (start us, length us, event | category | flops | bytes accessed | tf_op | source)
XLA Modules:
  0.0 79.9 jit_solution(2910040017424126416)
XLA Ops:
  0.0 0.6 maximum_bitcast_fusion.frequency_ref
  0.6 77.6 %shard_map.64 = bf16[2,32,2048]{2,1,0:T(8,128)(2,1)} custom-call(f32[1,128]{1,0:T(1,128)} %maximum_bitcast_fusion.frequency_ref, s32[2]{0:T(128)} %source_ref.1, s32[2,128]{1,0:T(2,128)} %segment_ref.1, bf16[2,32,4096]{2,1,0:T(8,128)(2,1)} %tokens_ref.1, f32[1,4096]{1,0:T(1,128)} %gain_ref.1, bf16[1,4096,1536]{2,1,0:T(8,128)(2,1)} %qkv_hbm.1, ...), custom_call_target="tpu_custom_call" | custom-call | tf_op jit(solution)/shard_map/pallas_call | solution.py:427
  78.2 1.7 %copy.8 = bf16[2,32,2048]{2,1,0:T(8,128)(2,1)} copy(bf16[2,32,2048]{2,1,0:T(8,128)(2,1)} %shard_map.64) | data formatting | bytes 524288
  (1 shorter events, 0.0 us)

commit v2 on v1

--- a/solution.py
+++ b/solution.py
@@ -303,19 +303,28 @@
             key = rotate(projected[:, at : at + HD] * scale, p).astype(jnp.bfloat16)
             at = at + HD
             value = (projected[:, at : at + HD] * scale).astype(jnp.bfloat16)
+            queries = jnp.concatenate(
+                [
+                    rotate(
+                        projected[:, base + h * HD : base + (h + 1) * HD] * scale, p
+                    ).astype(jnp.bfloat16)
+                    for h in range(GROUP)
+                ],
+                axis=0,
+            )
+            scores = lax.dot_general(
+                queries, key, (((1,), (1,)), ((), ())), preferred_element_type=jnp.float32
+            )
+            masked = jnp.concatenate([bias[p]] * GROUP, axis=0)
+            scores = jnp.where(masked < 0.0, -1e30, scores * HD ** (-0.5))
+            terms = jnp.exp(scores - jnp.max(scores, axis=1, keepdims=True))
+            weights = (terms * (1.0 / jnp.sum(terms, axis=1, keepdims=True))).astype(jnp.bfloat16)
+            mixed = jnp.dot(weights, value, preferred_element_type=jnp.float32)
             for h in range(GROUP):
-                at = base + h * HD
-                query = rotate(projected[:, at : at + HD] * scale, p).astype(jnp.bfloat16)
-                scores = lax.dot_general(
-                    query, key, (((1,), (1,)), ((), ())), preferred_element_type=jnp.float32
+                at = (g * GROUP + h) * HD
+                attended[:, at : at + HD] = mixed[h * length : (h + 1) * length, :].astype(
+                    jnp.bfloat16
                 )
-                scores = jnp.where(bias[p] < 0.0, -1e30, scores * HD ** (-0.5))
-                terms = jnp.exp(scores - jnp.max(scores, axis=1, keepdims=True))
-                weights = (terms / jnp.sum(terms, axis=1, keepdims=True)).astype(jnp.bfloat16)
-                at = (g * GROUP + h) * HD
-                attended[:, at : at + HD] = jnp.dot(
-                    weights, value, preferred_element_type=jnp.float32
-                ).astype(jnp.bfloat16)
 
         @pl.loop(0, CHUNKS)
         def _(c):

time: 80 us -> 73.6 us (0.920)
  Pallas kernels: 77.6 us -> 71.2 us
    pallas_call x1, Pallas kernels: 77.6 us -> 71.2 us  [on_device(): pl.pallas_call(functools.partial(kernel, dp_count, tensor_count), out_sha...]
where the time goes in v2:
time: 73.6 us; the launch traced here: 73.5 us
  Pallas kernels  71.2 us (97%)
  local copies, waits for them, and re-layouts  1.67 us (2%)
    pallas_call x1, Pallas kernels, on_device(): pl.pallas_call(functools.partial(kernel, dp_count, tensor_count), out_sha...  71.2 us
    unnamed x1, local copies, waits for them, and re-layouts  1.67 us

profile of v2, /device:TPU:1, one launch (start us, length us, event | category | flops | bytes accessed | tf_op | source)
XLA Modules:
  0.0 73.5 jit_solution(3516582251681341399)
XLA Ops:
  0.0 0.6 maximum_bitcast_fusion.frequency_ref
  0.6 71.2 %shard_map.64 = bf16[2,32,2048]{2,1,0:T(8,128)(2,1)} custom-call(f32[1,128]{1,0:T(1,128)} %maximum_bitcast_fusion.frequency_ref, s32[2]{0:T(128)} %source_ref.1, s32[2,128]{1,0:T(2,128)} %segment_ref.1, bf16[2,32,4096]{2,1,0:T(8,128)(2,1)} %tokens_ref.1, f32[1,4096]{1,0:T(1,128)} %gain_ref.1, bf16[1,4096,1536]{2,1,0:T(8,128)(2,1)} %qkv_hbm.1, ...), custom_call_target="tpu_custom_call" | custom-call | tf_op jit(solution)/shard_map/pallas_call | solution.py:436
  71.8 1.7 %copy.8 = bf16[2,32,2048]{2,1,0:T(8,128)(2,1)} copy(bf16[2,32,2048]{2,1,0:T(8,128)(2,1)} %shard_map.64) | data formatting | bytes 524288
  (1 shorter events, 0.0 us)

commit v3 on v2

--- a/solution.py
+++ b/solution.py
@@ -1,4 +1,5 @@
 import functools
+import math
 
 import jax
 import jax.numpy as jnp
@@ -18,7 +19,6 @@
 def kernel(
     dp_count,
     tensor_count,
-    frequency_ref,
     source_ref,
     segment_ref,
     tokens_ref,
@@ -182,10 +182,11 @@
                 sent_packs[c, target] = choose(target)
                 pack_copy(c, off).start()
 
-    freq = frequency_ref[0:1, :]
     row_id = lax.broadcasted_iota(jnp.int32, (length, length), 0)
     column_id = lax.broadcasted_iota(jnp.int32, (length, length), 1)
     lane = lax.broadcasted_iota(jnp.int32, (length, HD), 1)
+    pair = (lax.broadcasted_iota(jnp.int32, (1, HD), 1) % (HD // 2)).astype(jnp.float32)
+    freq = jnp.exp(pair * (-2.0 * math.log(ROPE_BASE) / HD))
     for p in range(micro):
         own = meta[z, micro + p : micro + p + 1, :]
 
@@ -227,7 +228,7 @@
                 gathered[p, c, pl.ds(pl.multiple_of(me * rows, rows), rows), :] = picked.astype(
                     jnp.bfloat16
                 )
-                for off in range(1, tensor_count):
+                for off in range(tensor_count - 1, 0, -1):
                     gather_copy(p, c, off).start()
 
     for copy in weight_copies:
@@ -266,7 +267,7 @@
             def _():
                 next_copy(p, c, 0).wait_recv()
 
-            for off in range(1, tensor_count):
+            for off in range(tensor_count - 1, 0, -1):
                 gather_copy(p, c, off).wait_recv()
             block = gathered[p, c].astype(jnp.float32)
             squares = jnp.sum(block * block, axis=1, keepdims=True)
@@ -335,7 +336,7 @@
                     weight_out[c, :, n : n + tile],
                     preferred_element_type=jnp.float32,
                 ).astype(jnp.bfloat16)
-            for off in range(1, tensor_count):
+            for off in range(tensor_count - 1, 0, -1):
                 sum_remote(p, c, off).start()
 
             @pl.when(section * (c // half) == section)
@@ -371,7 +372,7 @@
                 after = hidden[p, c] + add_up(p, c)
                 hidden[p, c] = after
                 hidden_low[p, c] = after.astype(jnp.bfloat16)
-                for off in range(tensor_count):
+                for off in range(tensor_count - 1, -1, -1):
                     next_copy(p, c, off).start()
 
     @pl.when(section == 1)
@@ -394,7 +395,7 @@
     def _(p):
         @pl.loop(0, CHUNKS)
         def _(c):
-            for off in range(1, tensor_count):
+            for off in range(tensor_count - 1, 0, -1):
                 sum_remote(p, c, off).wait_send()
 
             @pl.when(section * (c // half) != section)
@@ -403,9 +404,9 @@
 
             @pl.when(section == 0)
             def _():
-                for off in range(1, tensor_count):
+                for off in range(tensor_count - 1, 0, -1):
                     gather_copy(p, c, off).wait_send()
-                for off in range(tensor_count):
+                for off in range(tensor_count - 1, -1, -1):
                     next_copy(p, c, off).wait_send()
 
     @pl.when(section == 0)
@@ -426,9 +427,6 @@
     columns = qkv_weight.shape[2]
     depth = out_weight.shape[1]
     places = CHUNKS + CHUNKS // 2
-    exponent = jnp.arange(0, HD, 2, dtype=jnp.float32) / HD
-    frequency = ROPE_BASE ** (-exponent)
-    frequency = jnp.concatenate([frequency, frequency])[None, :]
     vmem = pl.BlockSpec(memory_space=pltpu.VMEM)
     anywhere = pl.BlockSpec(memory_space=pl.ANY)
     dma = pltpu.SemaphoreType.DMA
@@ -437,7 +435,6 @@
         functools.partial(kernel, dp_count, tensor_count),
         out_shape=jax.ShapeDtypeStruct((micro, rows, width // 2), bf16),
         in_specs=[
-            vmem,
             pl.BlockSpec(memory_space=pltpu.SMEM),
             vmem,
             vmem,
@@ -478,7 +475,7 @@
         compiler_params=pltpu.CompilerParams(
             collective_id=0, has_side_effects=True, vmem_limit_bytes=58 * 1024 * 1024
         ),
-    )(frequency, pack_source, segment, tokens, norm_gain, qkv_weight, out_weight)
+    )(pack_source, segment, tokens, norm_gain, qkv_weight, out_weight)
 
 
 def solution(mesh):

time: 73.6 us -> 72.9 us (level)
  no operation moved by 1% of the time
where the time goes in v3:
time: 72.9 us; the launch traced here: 72.8 us
  Pallas kernels  71.1 us (98%)
  local copies, waits for them, and re-layouts  1.67 us (2%)
    pallas_call x1, Pallas kernels, on_device(): pl.pallas_call(functools.partial(kernel, dp_count, tensor_count), out_sha...  71.1 us
    unnamed x1, local copies, waits for them, and re-layouts  1.67 us

profile of v3, /device:TPU:1, one launch (start us, length us, event | category | flops | bytes accessed | tf_op | source)
XLA Modules:
  0.0 72.8 jit_solution(11612324439049575184)
XLA Ops:
  0.0 71.1 %shard_map.64 = bf16[2,32,2048]{2,1,0:T(8,128)(2,1)} custom-call(s32[2]{0:T(128)} %source_ref.1, s32[2,128]{1,0:T(2,128)} %segment_ref.1, bf16[2,32,4096]{2,1,0:T(8,128)(2,1)} %tokens_ref.1, f32[1,4096]{1,0:T(1,128)} %gain_ref.1, bf16[1,4096,1536]{2,1,0:T(8,128)(2,1)} %qkv_hbm.1, bf16[1,1024,4096]{2,1,0:T(8,128)(2,1)} %out_hbm.1), custom_call_target="tpu_custom_call" | custom-call | tf_op jit(solution)/shard_map/pallas_call | solution.py:434
  71.1 1.7 %copy.8 = bf16[2,32,2048]{2,1,0:T(8,128)(2,1)} copy(bf16[2,32,2048]{2,1,0:T(8,128)(2,1)} %shard_map.64) | data formatting | bytes 524288
